TPU v7x, 32 devices: a whole 2x2x4 slice. The times are simulated.
32 devices in a mesh: dp: 8 (over y, x, core), mp: 4 (over z).
Axes of the slice: x: 2, y: 2, z: 4, core: 2. Of those that a mesh axis runs over, the one named last changes fastest.
Arguments:
- tokens: bfloat16 [32768, 768], P(('dp', 'mp')), may hold values from -6 to 6
- segment_ids: int32 [32768], P('dp'), may hold values from 0 to 1, as said below
- row_ends: int32 [128], P('dp'), may hold values from 127 to 255, as said below
- type_rows: bfloat16 [2, 768], replicated, may hold values from -3 to 3
- ln1_gain: float32 [768], replicated, may hold values from 0.1 to 1.9
- attn_qkv: bfloat16 [3, 768, 768], P(None, None, 'mp'), may hold values from -0.21875 to 0.21875
- attn_out: bfloat16 [768, 768], P('mp'), may hold values from -2.5 to 2.5
- ffn_up: bfloat16 [768, 3072], P(None, 'mp'), may hold values from -0.21875 to 0.21875
- ffn_down: bfloat16 [3072, 768], P('mp'), may hold values from -0.109375 to 0.109375
- adapter_down: bfloat16 [16, 768, 48], replicated, may hold values from -0.21875 to 0.21875
- adapter_up: bfloat16 [16, 48, 768], replicated, may hold values from -3 to 3
- ln2_gain: float32 [768], replicated, may hold values from 0.1 to 1.9
- joining_query: bfloat16 [768, 768], P(None, ('dp', 'mp')), may hold values from -0.21875 to 0.21875
- joining_key: bfloat16 [768, 768], P(None, ('dp', 'mp')), may hold values from -0.02734375 to 0.02734375
- joining_value: bfloat16 [768, 768], P(None, ('dp', 'mp')), may hold values from -0.4375 to 0.4375
- query_bias: bfloat16 [768], P(('dp', 'mp')), may hold values from -3 to 3
- cotangent: bfloat16 [32768, 768], P(('dp', 'mp')), may hold values from -6 to 6
Outputs:
- layer_out: float32 [32768, 768], P(('dp', 'mp'))
- grad_input: float32 [32768, 768], P(('dp', 'mp'))
- grad_query: float32 [768, 768], P(None, ('dp', 'mp'))
- grad_key: float32 [768, 768], P(None, ('dp', 'mp'))
- grad_value: float32 [768, 768], P(None, ('dp', 'mp'))
- grad_bias: float32 [768], P(('dp', 'mp'))
Inputs may be any that keep to these rules, and one draw needn't show every extreme that they name: A row's tokens after row_ends are padding; segment_ids is 1 from just after a row's first separator (at a position of 1 or more before row_ends) through row_ends and 0 elsewhere; some row ends at 255 and some at 127. `segment_ids`: consistent with row_ends as stated there.
All inputs are finite; a program needn't handle non-finite values.
Results may differ from a plain program's by a relative error of at most 0.034.
Values may be sent and summed in bfloat16 or wider, within the bound.
A program may use at most 256 MiB of HBM per device.

v0:
```python
from functools import partial

import jax
import jax.numpy as jnp
from jax import lax
from jax.sharding import PartitionSpec as P

D = 768
HEAD = 64
MICRO = 4


eps = 1e-06


def exact_gelu(values):
    return jax.nn.gelu(values, approximate=False)


def layer_norm(values, gain):
    center = values - jnp.mean(values, axis=-1, keepdims=True)
    spread = jnp.mean(center * center, axis=-1, keepdims=True)
    return gain * (center * lax.rsqrt(spread + eps))


def masked_scores(pieces, seq_ends, head_size):
    seq_len = pieces.shape[1]
    scores = jnp.einsum(
        "sqhd,skhd->shqk", pieces[:, :, 0], pieces[:, :, 1], preferred_element_type=jnp.float32
    ) * head_size ** (-0.5)
    places = lax.broadcasted_iota(jnp.int32, (1, 1, 1, seq_len), 3)
    return jnp.where(places <= seq_ends[:, None, None, None], scores, -1e30)


def attend(projected, seq_ends, head_count):
    total_rows = projected.shape[0]
    col_width = projected.shape[1] // 3
    head_size = col_width // head_count
    seq_count = seq_ends.shape[0]
    pieces = projected.reshape(seq_count, total_rows // seq_count, 3, head_count, head_size)
    scores = masked_scores(pieces, seq_ends, head_size)
    highest = jnp.max(scores, axis=-1, keepdims=True)
    log_total = highest + jnp.log(jnp.sum(jnp.exp(scores - highest), axis=-1, keepdims=True))
    attn_probs = jnp.exp(scores - log_total).astype(jnp.bfloat16)
    context = jnp.einsum(
        "shqk,skhd->sqhd", attn_probs, pieces[:, :, 2], preferred_element_type=jnp.float32
    )
    return (context.astype(jnp.bfloat16).reshape(total_rows, col_width), log_total)


def attend_back(projected, seq_ends, head_count, log_total, grad_context):
    total_rows = projected.shape[0]
    col_width = projected.shape[1] // 3
    head_size = col_width // head_count
    seq_count = seq_ends.shape[0]
    factor = head_size ** (-0.5)
    pieces = projected.reshape(seq_count, total_rows // seq_count, 3, head_count, head_size)
    attn_probs = jnp.exp(masked_scores(pieces, seq_ends, head_size) - log_total)
    grad_ctx = grad_context.reshape(seq_count, total_rows // seq_count, head_count, head_size)
    grad_probs = jnp.einsum(
        "sqhd,skhd->shqk", grad_ctx, pieces[:, :, 2], preferred_element_type=jnp.float32
    )
    grad_vals = jnp.einsum(
        "shqk,sqhd->skhd",
        attn_probs.astype(jnp.bfloat16),
        grad_ctx,
        preferred_element_type=jnp.float32,
    ).astype(jnp.bfloat16)
    grad_scores = (
        attn_probs * (grad_probs - jnp.sum(attn_probs * grad_probs, axis=-1, keepdims=True))
    ).astype(jnp.bfloat16)
    grad_queries = (
        jnp.einsum(
            "shqk,skhd->sqhd", grad_scores, pieces[:, :, 1], preferred_element_type=jnp.float32
        )
        * factor
    ).astype(jnp.bfloat16)
    grad_keys = (
        jnp.einsum(
            "shqk,sqhd->skhd", grad_scores, pieces[:, :, 0], preferred_element_type=jnp.float32
        )
        * factor
    ).astype(jnp.bfloat16)
    return jnp.stack((grad_queries, grad_keys, grad_vals), axis=2).reshape(
        total_rows, 3 * col_width
    )


def joining_step(merged, cot_rows, fetched, adapter_down, adapter_up, ln2_gain):
    query_mat, key_mat, value_mat, bias_full = fetched
    factor = D ** (-0.5)
    merged_low = merged.astype(jnp.bfloat16)
    adapt_pre = jnp.einsum(
        "rd,adb->rab", merged_low, adapter_down, preferred_element_type=jnp.float32
    )
    adapt_mid, adapt_back = jax.vjp(exact_gelu, adapt_pre)
    adapt_mid = adapt_mid.astype(jnp.bfloat16)
    adapted = (
        merged[:, None, :]
        + jnp.einsum("rab,abd->rad", adapt_mid, adapter_up, preferred_element_type=jnp.float32)
    ).astype(jnp.bfloat16)
    query_rows = (
        jnp.dot(merged_low, query_mat, preferred_element_type=jnp.float32)
        + bias_full.astype(jnp.float32)[None, :]
    ).astype(jnp.bfloat16)
    keyed = jnp.einsum("rd,ed->re", query_rows, key_mat, preferred_element_type=jnp.float32).astype(
        jnp.bfloat16
    )
    joining_scores = (
        jnp.einsum("re,rae->ra", keyed, adapted, preferred_element_type=jnp.float32) * factor
    )
    joining_probs = jax.nn.softmax(joining_scores, axis=-1)
    probs_low = joining_probs.astype(jnp.bfloat16)
    mixed = jnp.einsum("ra,rad->rd", probs_low, adapted, preferred_element_type=jnp.float32).astype(
        jnp.bfloat16
    )
    combined = merged + jnp.dot(mixed, value_mat, preferred_element_type=jnp.float32)
    layer_out, norm_back = jax.vjp(lambda inside: layer_norm(inside, ln2_gain), combined)
    grad_comb = norm_back(cot_rows.astype(jnp.float32))[0]
    grad_joined = grad_comb.astype(jnp.bfloat16)
    grad_value = jnp.einsum("rd,re->de", mixed, grad_joined, preferred_element_type=jnp.float32)
    grad_mixed = jnp.einsum("re,de->rd", grad_joined, value_mat, preferred_element_type=jnp.float32)
    grad_probs = jnp.einsum("rd,rad->ra", grad_mixed, adapted, preferred_element_type=jnp.float32)
    grad_scores = joining_probs * (
        grad_probs - jnp.sum(joining_probs * grad_probs, axis=-1, keepdims=True)
    )
    grad_adapted = (
        probs_low.astype(jnp.float32)[:, :, None] * grad_mixed[:, None, :]
        + (grad_scores * factor)[:, :, None] * keyed.astype(jnp.float32)[:, None, :]
    ).astype(jnp.bfloat16)
    grad_keyed = (
        jnp.einsum("ra,rad->rd", grad_scores, adapted, preferred_element_type=jnp.float32) * factor
    ).astype(jnp.bfloat16)
    grad_key = jnp.einsum("re,rd->ed", grad_keyed, query_rows, preferred_element_type=jnp.float32)
    grad_qrows = jnp.dot(grad_keyed, key_mat, preferred_element_type=jnp.float32).astype(
        jnp.bfloat16
    )
    grad_query = jnp.einsum("rd,re->de", merged_low, grad_qrows, preferred_element_type=jnp.float32)
    grad_bias = jnp.sum(grad_qrows.astype(jnp.float32), axis=0)
    grad_mid = jnp.einsum(
        "rad,abd->rab", grad_adapted, adapter_up, preferred_element_type=jnp.float32
    )
    grad_pre = adapt_back(grad_mid)[0].astype(jnp.bfloat16)
    grad_merged = (
        grad_comb
        + jnp.sum(grad_adapted.astype(jnp.float32), axis=1)
        + jnp.einsum("re,de->rd", grad_qrows, query_mat, preferred_element_type=jnp.float32)
        + jnp.einsum("rab,adb->rd", grad_pre, adapter_down, preferred_element_type=jnp.float32)
    )
    return (layer_out, grad_merged, (grad_query, grad_key, grad_value, grad_bias))


def frozen_micro(row_block, seq_ends, weights, movers, ln1_gain, finisher):
    flat_qkv, out_mat, up_mat, down_mat = weights
    (
        spread_in,
        sum_attn,
        spread_ffn,
        sum_ffn,
        spread_ffn_back,
        sum_up_back,
        spread_attn_back,
        sum_in_back,
    ) = movers
    head_count = flat_qkv.shape[1] // 3 // HEAD
    slice_len = row_block.shape[0]

    def project(shard_rows, offset):
        return jnp.dot(shard_rows, flat_qkv, preferred_element_type=jnp.float32).astype(
            jnp.bfloat16
        )

    projected = spread_in(row_block.astype(jnp.bfloat16), project)
    context, log_total = attend(projected, seq_ends, head_count)

    def out_terms(offset, amount):
        return jnp.dot(context, out_mat, preferred_element_type=jnp.float32)

    attended = sum_attn(out_terms, slice_len)
    hidden_one, norm_back = jax.vjp(
        lambda inside: layer_norm(inside, ln1_gain), row_block + attended
    )

    def widen(shard_rows, offset):
        return jnp.dot(shard_rows, up_mat, preferred_element_type=jnp.float32)

    widened = spread_ffn(hidden_one.astype(jnp.bfloat16), widen)
    activated, gelu_back = jax.vjp(exact_gelu, widened)
    activated = activated.astype(jnp.bfloat16)

    def down_terms(offset, amount):
        return jnp.dot(activated, down_mat, preferred_element_type=jnp.float32)

    merged = hidden_one + sum_ffn(down_terms, slice_len)
    layer_out, grad_merged, joining_terms = finisher(merged)

    def hidden_back(shard_rows, offset):
        return jnp.einsum("rd,fd->rf", shard_rows, down_mat, preferred_element_type=jnp.float32)

    grad_act = spread_ffn_back(grad_merged.astype(jnp.bfloat16), hidden_back)
    grad_wide = gelu_back(grad_act)[0].astype(jnp.bfloat16)

    def up_terms(offset, amount):
        return jnp.einsum("rf,df->rd", grad_wide, up_mat, preferred_element_type=jnp.float32)

    grad_hidden = grad_merged + sum_up_back(up_terms, slice_len)
    grad_summed = norm_back(grad_hidden)[0]

    def context_back(shard_rows, offset):
        return jnp.einsum(
            "rd,cd->rc", shard_rows, out_mat, preferred_element_type=jnp.float32
        ).astype(jnp.bfloat16)

    grad_context = spread_attn_back(grad_summed.astype(jnp.bfloat16), context_back)
    grad_proj = attend_back(projected, seq_ends, head_count, log_total, grad_context)

    def in_terms(offset, amount):
        return jnp.einsum("rc,dc->rd", grad_proj, flat_qkv, preferred_element_type=jnp.float32)

    grad_rows = grad_summed + sum_in_back(in_terms, slice_len)
    return (layer_out, grad_rows, joining_terms)


def local(
    tokens,
    segment_ids,
    row_ends,
    type_rows,
    ln1_gain,
    attn_qkv,
    attn_out,
    ffn_up,
    ffn_down,
    adapter_down,
    adapter_up,
    ln2_gain,
    joining_query,
    joining_key,
    joining_value,
    query_bias,
    cotangent,
):
    model_parts = lax.axis_size("mp")
    my_part = lax.axis_index("mp")
    own_rows = tokens.shape[0]
    slice_rows = own_rows // MICRO
    group_seqs = row_ends.shape[0]
    own_seqs = group_seqs // model_parts
    micro_seqs = own_seqs // MICRO
    own_types = lax.dynamic_slice_in_dim(segment_ids, my_part * own_rows, own_rows)
    group_ends = row_ends.reshape(model_parts, MICRO, micro_seqs)
    type_float = type_rows.astype(jnp.float32)
    summed_all = tokens.astype(jnp.float32) + jnp.where(
        own_types[:, None] == 1, type_float[1][None, :], type_float[0][None, :]
    )
    flat_qkv = jnp.transpose(attn_qkv, (1, 0, 2)).reshape(attn_qkv.shape[1], -1)
    weights = (flat_qkv, attn_out, ffn_up, ffn_down)
    movers = (
        lambda values, mapper: mapper(
            lax.all_gather(values, "mp", axis=0, tiled=True), jnp.int32(0)
        ),
        lambda producer, amount: lax.psum_scatter(
            producer(jnp.int32(0), amount * lax.axis_size("mp")),
            "mp",
            scatter_dimension=0,
            tiled=True,
        ),
        lambda values, mapper: mapper(
            lax.all_gather(values, "mp", axis=0, tiled=True), jnp.int32(0)
        ),
        lambda producer, amount: lax.psum_scatter(
            producer(jnp.int32(0), amount * lax.axis_size("mp")),
            "mp",
            scatter_dimension=0,
            tiled=True,
        ),
        lambda values, mapper: mapper(
            lax.all_gather(values, "mp", axis=0, tiled=True), jnp.int32(0)
        ),
        lambda producer, amount: lax.psum_scatter(
            producer(jnp.int32(0), amount * lax.axis_size("mp")),
            "mp",
            scatter_dimension=0,
            tiled=True,
        ),
        lambda values, mapper: mapper(
            lax.all_gather(values, "mp", axis=0, tiled=True), jnp.int32(0)
        ),
        lambda producer, amount: lax.psum_scatter(
            producer(jnp.int32(0), amount * lax.axis_size("mp")),
            "mp",
            scatter_dimension=0,
            tiled=True,
        ),
    )
    ends_for = lambda micro_index: group_ends[:, micro_index, :].reshape(-1)
    width = tokens.shape[1]
    totals = (
        jnp.zeros((width, width), jnp.float32),
        jnp.zeros((width, width), jnp.float32),
        jnp.zeros((width, width), jnp.float32),
        jnp.zeros((width,), jnp.float32),
    )
    out_parts = []
    grad_parts = []
    for micro_index in range(MICRO):
        fetched = (
            lax.all_gather(joining_query, ("dp", "mp"), axis=1, tiled=True),
            lax.all_gather(joining_key, ("dp", "mp"), axis=1, tiled=True),
            lax.all_gather(joining_value, ("dp", "mp"), axis=1, tiled=True),
            lax.all_gather(query_bias, ("dp", "mp"), axis=0, tiled=True),
        )
        row_block = summed_all[micro_index * slice_rows : (micro_index + 1) * slice_rows]
        cot_block = cotangent[micro_index * slice_rows : (micro_index + 1) * slice_rows]
        finisher = partial(
            joining_step,
            cot_rows=cot_block,
            fetched=fetched,
            adapter_down=adapter_down,
            adapter_up=adapter_up,
            ln2_gain=ln2_gain,
        )
        layer_part, grad_part, joining_terms = frozen_micro(
            row_block, ends_for(micro_index), weights, movers, ln1_gain, finisher
        )
        out_parts.append(layer_part)
        grad_parts.append(grad_part)
        totals = tuple((total + term for total, term in zip(totals, joining_terms)))
    shards = (
        lax.psum_scatter(totals[0], ("dp", "mp"), scatter_dimension=1, tiled=True),
        lax.psum_scatter(totals[1], ("dp", "mp"), scatter_dimension=1, tiled=True),
        lax.psum_scatter(totals[2], ("dp", "mp"), scatter_dimension=1, tiled=True),
        lax.psum_scatter(totals[3], ("dp", "mp"), scatter_dimension=0, tiled=True),
    )
    layer_out = jnp.concatenate(out_parts, axis=0)
    grad_input = jnp.concatenate(grad_parts, axis=0)
    return (layer_out, grad_input, shards[0], shards[1], shards[2], shards[3])


def solution(mesh):
    in_specs = (
        P(("dp", "mp"), None),
        P("dp"),
        P("dp"),
        P(),
        P(),
        P(None, None, "mp"),
        P("mp", None),
        P(None, "mp"),
        P("mp", None),
        P(),
        P(),
        P(),
        P(None, ("dp", "mp")),
        P(None, ("dp", "mp")),
        P(None, ("dp", "mp")),
        P(("dp", "mp")),
        P(("dp", "mp"), None),
    )
    out_specs = (
        P(("dp", "mp"), None),
        P(("dp", "mp"), None),
        P(None, ("dp", "mp")),
        P(None, ("dp", "mp")),
        P(None, ("dp", "mp")),
        P(("dp", "mp")),
    )
    return jax.shard_map(local, mesh=mesh, in_specs=in_specs, out_specs=out_specs, check_vma=False)
```

profile of v0, /device:TPU:0, one launch (start us, length us, event | category | flops | bytes accessed | tf_op | source)
XLA Modules:
  0.0 2271.8 jit_solution(18045153296948872997)
XLA Ops:
  15.9 37.4 %all-gather.20.cloned.1.call-done = bf16[1024,768]{1,0:T(8,128)(2,1)} async-done(((bf16[256,768]{1,0:T(8,128)(2,1)}), bf16[1024,768]{1,0:T(8,128)(2,1)}) %all-gather.20.cloned.1.call-update) | async-done | bytes 1572880 | tf_op jit(solution)/shard_map/all_gather | solution.py:260
  63.5 28.0 %all-gather.34.cloned.1.call-done = bf16[1024,768]{1,0:T(8,128)(2,1)} async-done(((bf16[256,768]{1,0:T(8,128)(2,1)}), bf16[1024,768]{1,0:T(8,128)(2,1)}) %all-gather.34.cloned.1.call-update) | async-done | bytes 1572880 | tf_op jit(solution)/shard_map/all_gather | solution.py:260
  104.6 24.5 %all-gather.38.cloned.1.call-done = bf16[1024,768]{1,0:T(8,128)(2,1)} async-done(((bf16[256,768]{1,0:T(8,128)(2,1)}), bf16[1024,768]{1,0:T(8,128)(2,1)}) %all-gather.38.cloned.1.call-update) | async-done | bytes 1572880 | tf_op jit(solution)/shard_map/all_gather | solution.py:260
  142.0 24.5 %all-gather.30.cloned.1.call-done = bf16[1024,768]{1,0:T(8,128)(2,1)} async-done(((bf16[256,768]{1,0:T(8,128)(2,1)}), bf16[1024,768]{1,0:T(8,128)(2,1)}) %all-gather.30.cloned.1.call-update) | async-done | bytes 1572880 | tf_op jit(solution)/shard_map/all_gather | solution.py:260
  179.4 48.4 %reduce-scatter.20.cloned.1.call-done = f32[256,768]{1,0:T(8,128)} async-done(((f32[1024,768]{1,0:T(8,128)}), f32[256,768]{1,0:T(8,128)}) %reduce-scatter.20.cloned.1.call-update) | async-done | bytes 786448 | tf_op jit(solution)/shard_map/reduce_scatter | solution.py:262
  227.8 62.5 %reduce-scatter.28.cloned.1.call-done = f32[256,768]{1,0:T(8,128)} async-done(((f32[1024,768]{1,0:T(8,128)}), f32[256,768]{1,0:T(8,128)}) %reduce-scatter.28.cloned.1.call-update) | async-done | bytes 786448 | tf_op jit(solution)/shard_map/reduce_scatter | solution.py:262
  290.2 62.6 %reduce-scatter.32.cloned.1.call-done = f32[256,768]{1,0:T(8,128)} async-done(((f32[1024,768]{1,0:T(8,128)}), f32[256,768]{1,0:T(8,128)}) %reduce-scatter.32.cloned.1.call-update) | async-done | bytes 786448 | tf_op jit(solution)/shard_map/reduce_scatter | solution.py:262
  352.9 63.2 %reduce-scatter.24.cloned.1.call-done = f32[256,768]{1,0:T(8,128)} async-done(((f32[1024,768]{1,0:T(8,128)}), f32[256,768]{1,0:T(8,128)}) %reduce-scatter.24.cloned.1.call-update) | async-done | bytes 786448 | tf_op jit(solution)/shard_map/reduce_scatter | solution.py:262
  423.9 36.2 %all-gather.22.cloned.1.call-done = bf16[1024,768]{1,0:T(8,128)(2,1)} async-done(((bf16[256,768]{1,0:T(8,128)(2,1)}), bf16[1024,768]{1,0:T(8,128)(2,1)}) %all-gather.22.cloned.1.call-update) | async-done | bytes 1572880 | tf_op jit(solution)/shard_map/all_gather | solution.py:269
  460.2 9.0 fusion.56
  475.0 23.2 %all-gather.32.cloned.1.call-done = bf16[1024,768]{1,0:T(8,128)(2,1)} async-done(((bf16[256,768]{1,0:T(8,128)(2,1)}), bf16[1024,768]{1,0:T(8,128)(2,1)}) %all-gather.32.cloned.1.call-update) | async-done | bytes 1572880 | tf_op jit(solution)/shard_map/all_gather | solution.py:269
  498.1 9.0 fusion.57
  516.6 43.6 %reduce-scatter.22.cloned.1.call-done = f32[256,768]{1,0:T(8,128)} async-done(((f32[1024,768]{1,0:T(8,128)}), f32[256,768]{1,0:T(8,128)}) %reduce-scatter.22.cloned.1.call-update) | async-done | bytes 786448 | tf_op jit(solution)/shard_map/reduce_scatter | solution.py:271
  560.2 63.1 %reduce-scatter.26.cloned.1.call-done = f32[256,768]{1,0:T(8,128)} async-done(((f32[1024,768]{1,0:T(8,128)}), f32[256,768]{1,0:T(8,128)}) %reduce-scatter.26.cloned.1.call-update) | async-done | bytes 786448 | tf_op jit(solution)/shard_map/reduce_scatter | solution.py:271
  629.3 34.7 %all-gather.40.cloned.1.call-done = bf16[1024,768]{1,0:T(8,128)(2,1)} async-done(((bf16[256,768]{1,0:T(8,128)(2,1)}), bf16[1024,768]{1,0:T(8,128)(2,1)}) %all-gather.40.cloned.1.call-update) | async-done | bytes 1572880 | tf_op jit(solution)/shard_map/all_gather | solution.py:269
  664.0 8.9 fusion.59
  679.6 39.2 %all-reduce = bf16[768]{0:T(1024)(128)(2,1)S(1)} all-reduce(bf16[768]{0:T(1024)(128)(2,1)S(1)} %dynamic-update-slice), channel_id=1, replica_groups=mesh['dp'=8,'mp'=4] {'dp','mp'}, use_global_device_ids=true, to_apply=%add | all-reduce | flops 768 | bytes 3072
  722.9 52.5 %all-gather.26.cloned.1.call-done = bf16[768,768]{0,1:T(8,128)(2,1)} async-done(((bf16[768,24]{0,1:T(8,128)(2,1)}), bf16[768,768]{0,1:T(8,128)(2,1)}) %all-gather.26.cloned.1.call-update) | async-done | bytes 1179664 | tf_op jit(solution)/shard_map/all_gather | solution.py:309
  778.3 35.2 %all-gather.36.cloned.1.call-done = bf16[1024,768]{1,0:T(8,128)(2,1)} async-done(((bf16[256,768]{1,0:T(8,128)(2,1)}), bf16[1024,768]{1,0:T(8,128)(2,1)}) %all-gather.36.cloned.1.call-update) | async-done | bytes 1572880 | tf_op jit(solution)/shard_map/all_gather | solution.py:269
  813.5 8.9 fusion.58
  860.1 7.7 fusion.52
  872.7 7.0 fusion.44
  881.7 49.4 %reduce-scatter.34.cloned.1.call-done = f32[256,768]{1,0:T(8,128)} async-done(((f32[1024,768]{1,0:T(8,128)}), f32[256,768]{1,0:T(8,128)}) %reduce-scatter.34.cloned.1.call-update) | async-done | bytes 786448 | tf_op jit(solution)/shard_map/reduce_scatter | solution.py:271
  931.1 63.2 %reduce-scatter.30.cloned.1.call-done = f32[256,768]{1,0:T(8,128)} async-done(((f32[1024,768]{1,0:T(8,128)}), f32[256,768]{1,0:T(8,128)}) %reduce-scatter.30.cloned.1.call-update) | async-done | bytes 786448 | tf_op jit(solution)/shard_map/reduce_scatter | solution.py:271
  1016.9 6.8 fusion.28
  1043.5 6.9 fusion.36
  1056.4 4.9 fusion.34
  1067.0 7.0 convolution_bitcast_fusion.1
  1074.0 4.6 convert_reduce_fusion.1
  1080.6 4.7 fusion.365
  1087.7 4.5 fusion.26
  1101.7 7.3 fusion.42
  1116.1 7.0 fusion.32
  1128.7 7.7 fusion.24
  1137.8 7.4 fusion.50
  1156.0 4.9 convert_reduce_fusion
  1160.9 7.0 convolution_bitcast_fusion
  1171.1 7.5 fusion.40
  1181.7 4.6 convert_reduce_fusion.2
  1186.3 7.1 convolution_bitcast_fusion.2
  1196.8 7.5 fusion.48
  1208.2 4.6 convert_reduce_fusion.3
  1212.8 7.0 convolution_bitcast_fusion.3
  1223.2 8.5 fusion.98
  1233.0 8.1 fusion.99
  1241.4 12.1 all-gather.46.cloned.1.call-done
  1253.5 8.0 fusion.97
  1261.6 29.5 %all-gather.42.cloned.1.call-done = bf16[1024,768]{1,0:T(8,128)(2,1)} async-done(((bf16[256,768]{1,0:T(8,128)(2,1)}), bf16[1024,768]{1,0:T(8,128)(2,1)}) %all-gather.42.cloned.1.call-update) | async-done | bytes 1572880 | tf_op jit(solution)/shard_map/all_gather | solution.py:278
  1291.1 8.0 fusion.96
  1299.2 53.1 %reduce-scatter.44.cloned.1.call-done = f32[256,768]{1,0:T(8,128)} async-done(((f32[1024,768]{1,0:T(8,128)}), f32[256,768]{1,0:T(8,128)}) %reduce-scatter.44.cloned.1.call-update) | async-done | bytes 786448 | tf_op jit(solution)/shard_map/reduce_scatter | solution.py:280
  1352.4 63.2 %reduce-scatter.48.cloned.1.call-done = f32[256,768]{1,0:T(8,128)} async-done(((f32[1024,768]{1,0:T(8,128)}), f32[256,768]{1,0:T(8,128)}) %reduce-scatter.48.cloned.1.call-update) | async-done | bytes 786448 | tf_op jit(solution)/shard_map/reduce_scatter | solution.py:280
  1415.6 62.5 %reduce-scatter.40.cloned.1.call-done = f32[256,768]{1,0:T(8,128)} async-done(((f32[1024,768]{1,0:T(8,128)}), f32[256,768]{1,0:T(8,128)}) %reduce-scatter.40.cloned.1.call-update) | async-done | bytes 786448 | tf_op jit(solution)/shard_map/reduce_scatter | solution.py:280
  1478.0 63.1 %reduce-scatter.36.cloned.1.call-done = f32[256,768]{1,0:T(8,128)} async-done(((f32[1024,768]{1,0:T(8,128)}), f32[256,768]{1,0:T(8,128)}) %reduce-scatter.36.cloned.1.call-update) | async-done | bytes 786448 | tf_op jit(solution)/shard_map/reduce_scatter | solution.py:280
  1559.1 27.8 %all-gather.44.cloned.1.call-done = bf16[1024,768]{1,0:T(8,128)(2,1)} async-done(((bf16[256,768]{1,0:T(8,128)(2,1)}), bf16[1024,768]{1,0:T(8,128)(2,1)}) %all-gather.44.cloned.1.call-update) | async-done | bytes 1572880 | tf_op jit(solution)/shard_map/all_gather | solution.py:287
  1600.4 24.7 %all-gather.52.cloned.1.call-done = bf16[1024,768]{1,0:T(8,128)(2,1)} async-done(((bf16[256,768]{1,0:T(8,128)(2,1)}), bf16[1024,768]{1,0:T(8,128)(2,1)}) %all-gather.52.cloned.1.call-update) | async-done | bytes 1572880 | tf_op jit(solution)/shard_map/all_gather | solution.py:287
  1638.5 24.5 %all-gather.56.cloned.1.call-done = bf16[1024,768]{1,0:T(8,128)(2,1)} async-done(((bf16[256,768]{1,0:T(8,128)(2,1)}), bf16[1024,768]{1,0:T(8,128)(2,1)}) %all-gather.56.cloned.1.call-update) | async-done | bytes 1572880 | tf_op jit(solution)/shard_map/all_gather | solution.py:287
  1676.6 24.1 %all-gather.48.cloned.1.call-done = bf16[1024,768]{1,0:T(8,128)(2,1)} async-done(((bf16[256,768]{1,0:T(8,128)(2,1)}), bf16[1024,768]{1,0:T(8,128)(2,1)}) %all-gather.48.cloned.1.call-update) | async-done | bytes 1572880 | tf_op jit(solution)/shard_map/all_gather | solution.py:287
  1730.8 42.5 %all-reduce.1 = f32[768]{0:T(1024)S(1)} all-reduce(f32[768]{0:T(1024)S(1)} %add_add_fusion.15), channel_id=21, replica_groups=mesh['dp'=8,'mp'=4] {'dp','mp'}, use_global_device_ids=true, to_apply=%region_83.84.clone | all-reduce | flops 768 | bytes 6144
  1779.6 45.9 %reduce-scatter.46.cloned.1.call-done = f32[256,768]{1,0:T(8,128)} async-done(((f32[1024,768]{1,0:T(8,128)}), f32[256,768]{1,0:T(8,128)}) %reduce-scatter.46.cloned.1.call-update) | async-done | bytes 786448 | tf_op jit(solution)/shard_map/reduce_scatter | solution.py:289
  1827.9 60.8 %reduce-scatter.50.cloned.1.call-done = f32[256,768]{1,0:T(8,128)} async-done(((f32[1024,768]{1,0:T(8,128)}), f32[256,768]{1,0:T(8,128)}) %reduce-scatter.50.cloned.1.call-update) | async-done | bytes 786448 | tf_op jit(solution)/shard_map/reduce_scatter | solution.py:289
  1890.8 60.5 %reduce-scatter.42.cloned.1.call-done = f32[256,768]{1,0:T(8,128)} async-done(((f32[1024,768]{1,0:T(8,128)}), f32[256,768]{1,0:T(8,128)}) %reduce-scatter.42.cloned.1.call-update) | async-done | bytes 786448 | tf_op jit(solution)/shard_map/reduce_scatter | solution.py:289
  1955.8 100.3 %reduce-scatter.56.cloned.1.call-done = f32[768,24]{0,1:T(8,128)} async-done(((f32[768,768]{0,1:T(8,128)}), f32[768,24]{0,1:T(8,128)}) %reduce-scatter.56.cloned.1.call-update) | async-done | bytes 73744 | tf_op jit(solution)/shard_map/reduce_scatter | solution.py:332
  2056.1 104.7 %reduce-scatter.54.cloned.1.call-done = f32[768,24]{0,1:T(8,128)} async-done(((f32[768,768]{0,1:T(8,128)}), f32[768,24]{0,1:T(8,128)}) %reduce-scatter.54.cloned.1.call-update) | async-done | bytes 73744 | tf_op jit(solution)/shard_map/reduce_scatter | solution.py:331
  2160.8 104.0 %reduce-scatter.52.cloned.1.call-done = f32[768,24]{0,1:T(8,128)} async-done(((f32[768,768]{0,1:T(8,128)}), f32[768,24]{0,1:T(8,128)}) %reduce-scatter.52.cloned.1.call-update) | async-done | bytes 73744 | tf_op jit(solution)/shard_map/reduce_scatter | solution.py:330
  (796 shorter events, 357.0 us)
Async XLA Ops:
  7.2 821.4 %copy-start = (bf16[16,48,768]{2,1,0:T(8,128)(2,1)S(1)}, bf16[16,48,768]{2,1,0:T(8,128)(2,1)}, u32[]{:S(2)}) copy-start(bf16[16,48,768]{2,1,0:T(8,128)(2,1)} %param.27) | copy-start | bytes 3538948
  7.2 46.2 %all-gather.20.cloned.1.call-start = ((), (), s32[]{:S(2)}) async-start(), calls=%async_computation.19 | async-start | bytes 1966080 | tf_op jit(solution)/shard_map/all_gather | solution.py:260
  13.4 78.1 %all-gather.34.cloned.1.call-start = ((), (), s32[]{:S(2)}) async-start(), calls=%async_computation.30 | async-start | bytes 1966080 | tf_op jit(solution)/shard_map/all_gather | solution.py:260
  14.2 114.9 %all-gather.38.cloned.1.call-start = ((), (), s32[]{:S(2)}) async-start(), calls=%async_computation.34 | async-start | bytes 1966080 | tf_op jit(solution)/shard_map/all_gather | solution.py:260
  14.9 151.6 %all-gather.30.cloned.1.call-start = ((), (), s32[]{:S(2)}) async-start(), calls=%async_computation.26 | async-start | bytes 1966080 | tf_op jit(solution)/shard_map/all_gather | solution.py:260
  15.5 212.3 %reduce-scatter.20.cloned.1.call-start = ((), (), s32[]{:S(2)}) async-start(), calls=%async_computation.20 | async-start | bytes 3932160 | tf_op jit(solution)/shard_map/reduce_scatter | solution.py:262
  15.9 159.7 %copy-start.179 = (pred[4,256]{1,0:T(4,128)(4,1)}, pred[4,256]{1,0:T(4,128)(4,1)S(1)}, u32[]{:S(2)}) copy-start(pred[4,256]{1,0:T(4,128)(4,1)S(1)} %get-tuple-element.164) | copy-start | bytes 3076
  63.4 226.8 %reduce-scatter.28.cloned.1.call-start = ((), (), s32[]{:S(2)}) async-start(), calls=%async_computation.31 | async-start | bytes 3932160 | tf_op jit(solution)/shard_map/reduce_scatter | solution.py:262
  63.5 74.7 %copy-start.181 = (pred[4,256]{1,0:T(4,128)(4,1)}, pred[4,256]{1,0:T(4,128)(4,1)S(1)}, u32[]{:S(2)}) copy-start(pred[4,256]{1,0:T(4,128)(4,1)S(1)} %get-tuple-element.162) | copy-start | bytes 3076
  104.3 248.6 %reduce-scatter.32.cloned.1.call-start = ((), (), s32[]{:S(2)}) async-start(), calls=%async_computation.35 | async-start | bytes 3932160 | tf_op jit(solution)/shard_map/reduce_scatter | solution.py:262
  141.9 274.1 %reduce-scatter.24.cloned.1.call-start = ((), (), s32[]{:S(2)}) async-start(), calls=%async_computation.27 | async-start | bytes 3932160 | tf_op jit(solution)/shard_map/reduce_scatter | solution.py:262
  179.3 242.4 %copy-start.148 = (f32[768]{0:T(1024)S(1)}, f32[768]{0:T(1024)}, u32[]{:S(2)}) copy-start(f32[768]{0:T(1024)} %param.21) | copy-start | bytes 9220
  179.3 280.9 %all-gather.22.cloned.1.call-start = ((), (), s32[]{:S(2)}) async-start(), calls=%async_computation.21 | async-start | bytes 1966080 | tf_op jit(solution)/shard_map/all_gather | solution.py:269
  419.8 203.4 %copy-start.16 = (f32[256,768]{1,0:T(8,128)}, f32[256,768]{1,0:T(8,128)S(1)}, u32[]{:S(2)}) copy-start(f32[256,768]{1,0:T(8,128)S(1)} %get-tuple-element.51) | copy-start | bytes 2359300
  419.8 203.4 %copy-start.18 = (f32[256,768]{1,0:T(8,128)}, f32[256,768]{1,0:T(8,128)S(1)}, u32[]{:S(2)}) copy-start(f32[256,768]{1,0:T(8,128)S(1)} %get-tuple-element.53) | copy-start | bytes 2359300
  419.8 203.4 %copy-start.20 = (f32[256,768]{1,0:T(8,128)}, f32[256,768]{1,0:T(8,128)S(1)}, u32[]{:S(2)}) copy-start(f32[256,768]{1,0:T(8,128)S(1)} %get-tuple-element.41) | copy-start | bytes 2359300
  419.8 203.4 %copy-start.168 = (f32[256]{0:T(256)}, f32[256]{0:T(256)S(1)}, u32[]{:S(2)}) copy-start(f32[256]{0:T(256)S(1)} %broadcast_multiply_fusion.9) | copy-start | bytes 3076
  419.8 203.4 %copy-start.170 = (f32[256]{0:T(256)}, f32[256]{0:T(256)S(1)}, u32[]{:S(2)}) copy-start(f32[256]{0:T(256)S(1)} %broadcast_multiply_fusion.11) | copy-start | bytes 3076
  422.9 75.3 %all-gather.32.cloned.1.call-start = ((), (), s32[]{:S(2)}) async-start(), calls=%async_computation.28 | async-start | bytes 1966080 | tf_op jit(solution)/shard_map/all_gather | solution.py:269
  423.5 136.7 %reduce-scatter.22.cloned.1.call-start = ((), (), s32[]{:S(2)}) async-start(), calls=%async_computation.22 | async-start | bytes 3932160 | tf_op jit(solution)/shard_map/reduce_scatter | solution.py:271
  474.9 148.3 %reduce-scatter.26.cloned.1.call-start = ((), (), s32[]{:S(2)}) async-start(), calls=%async_computation.29 | async-start | bytes 3932160 | tf_op jit(solution)/shard_map/reduce_scatter | solution.py:271
  512.9 151.1 %all-gather.40.cloned.1.call-start = ((), (), s32[]{:S(2)}) async-start(), calls=%async_computation.36 | async-start | bytes 1966080 | tf_op jit(solution)/shard_map/all_gather | solution.py:269
  513.7 113.1 %copy-start.172 = (f32[256]{0:T(256)}, f32[256]{0:T(256)S(1)}, u32[]{:S(2)}) copy-start(f32[256]{0:T(256)S(1)} %broadcast_multiply_fusion.5) | copy-start | bytes 3076
  626.8 92.9 %all-gather.24.cloned.1.call-start = ((), (), s32[]{:S(2)}) async-start(), calls=%async_computation.23 | async-start | bytes 1216512 | tf_op jit(solution)/shard_map/all_gather | solution.py:308
  627.4 148.1 %all-gather.26.cloned.1.call-start = ((), (), s32[]{:S(2)}) async-start(), calls=%async_computation.24 | async-start | bytes 1216512 | tf_op jit(solution)/shard_map/all_gather | solution.py:309
  627.9 185.5 %all-gather.36.cloned.1.call-start = ((), (), s32[]{:S(2)}) async-start(), calls=%async_computation.32 | async-start | bytes 1966080 | tf_op jit(solution)/shard_map/all_gather | solution.py:269
  628.5 240.6 %all-gather.28.cloned.1.call-start = ((), (), s32[]{:S(2)}) async-start(), calls=%async_computation.25 | async-start | bytes 1216512 | tf_op jit(solution)/shard_map/all_gather | solution.py:310
  629.1 46.5 %copy-start.47 = (bf16[768,768]{1,0:T(8,128)(2,1)S(1)}, bf16[768,768]{1,0:T(8,128)(2,1)}, u32[]{:S(2)}) copy-start(bf16[768,768]{1,0:T(8,128)(2,1)} %param.25) | copy-start | bytes 3538948
  629.1 302.0 %reduce-scatter.34.cloned.1.call-start = ((), (), s32[]{:S(2)}) async-start(), calls=%async_computation.37 | async-start | bytes 3932160 | tf_op jit(solution)/shard_map/reduce_scatter | solution.py:271
  678.8 315.5 %reduce-scatter.30.cloned.1.call-start = ((), (), s32[]{:S(2)}) async-start(), calls=%async_computation.33 | async-start | bytes 3932160 | tf_op jit(solution)/shard_map/reduce_scatter | solution.py:271
  718.8 59.5 %copy-start.158 = (f32[768]{0:T(1024)}, f32[768]{0:T(1024)S(1)}, u32[]{:S(2)}) copy-start(f32[768]{0:T(1024)S(1)} %convert_element_type.458) | copy-start | bytes 9220
  721.5 100.9 %copy-start.94 = (bf16[256,768]{1,0:T(8,128)(2,1)}, bf16[256,768]{1,0:T(8,128)(2,1)S(1)}, u32[]{:S(2)}) copy-start(bf16[256,768]{1,0:T(8,128)(2,1)S(1)} %fusion.108) | copy-start | bytes 1179652
  778.2 47.0 %copy-start.48 = (bf16[768,768]{1,0:T(8,128)(2,1)S(1)}, bf16[768,768]{1,0:T(8,128)(2,1)}, u32[]{:S(2)}) copy-start(bf16[768,768]{1,0:T(8,128)(2,1)} %param.25) | copy-start | bytes 3538948
  828.3 394.8 %all-gather.50.cloned.1.call-start = ((), (), s32[]{:S(2)}) async-start(), calls=%async_computation.46 | async-start | bytes 1966080 | tf_op jit(solution)/shard_map/all_gather | solution.py:278
  1125.9 105.9 %all-gather.54.cloned.1.call-start = ((), (), s32[]{:S(2)}) async-start(), calls=%async_computation.50 | async-start | bytes 1966080 | tf_op jit(solution)/shard_map/all_gather | solution.py:278
  1178.7 74.8 %all-gather.46.cloned.1.call-start = ((), (), s32[]{:S(2)}) async-start(), calls=%async_computation.42 | async-start | bytes 1966080 | tf_op jit(solution)/shard_map/all_gather | solution.py:278
  1204.3 86.8 %all-gather.42.cloned.1.call-start = ((), (), s32[]{:S(2)}) async-start(), calls=%async_computation.38 | async-start | bytes 1966080 | tf_op jit(solution)/shard_map/all_gather | solution.py:278
  1223.1 129.2 %reduce-scatter.44.cloned.1.call-start = ((), (), s32[]{:S(2)}) async-start(), calls=%async_computation.47 | async-start | bytes 3932160 | tf_op jit(solution)/shard_map/reduce_scatter | solution.py:280
  1231.7 183.8 %reduce-scatter.48.cloned.1.call-start = ((), (), s32[]{:S(2)}) async-start(), calls=%async_computation.51 | async-start | bytes 3932160 | tf_op jit(solution)/shard_map/reduce_scatter | solution.py:280
  1241.1 237.0 %reduce-scatter.40.cloned.1.call-start = ((), (), s32[]{:S(2)}) async-start(), calls=%async_computation.43 | async-start | bytes 3932160 | tf_op jit(solution)/shard_map/reduce_scatter | solution.py:280
  1261.6 279.5 %reduce-scatter.36.cloned.1.call-start = ((), (), s32[]{:S(2)}) async-start(), calls=%async_computation.39 | async-start | bytes 3932160 | tf_op jit(solution)/shard_map/reduce_scatter | solution.py:280
  1299.1 242.0 %copy-start.17 = (f32[256,768]{1,0:T(8,128)S(1)}, f32[256,768]{1,0:T(8,128)}, u32[]{:S(2)}) copy-start(f32[256,768]{1,0:T(8,128)} %copy-done.16) | copy-start | bytes 2359300
  1299.1 242.0 %copy-start.19 = (f32[256,768]{1,0:T(8,128)S(1)}, f32[256,768]{1,0:T(8,128)}, u32[]{:S(2)}) copy-start(f32[256,768]{1,0:T(8,128)} %copy-done.18) | copy-start | bytes 2359300
  1299.1 242.0 %copy-start.21 = (f32[256,768]{1,0:T(8,128)S(1)}, f32[256,768]{1,0:T(8,128)}, u32[]{:S(2)}) copy-start(f32[256,768]{1,0:T(8,128)} %copy-done.20) | copy-start | bytes 2359300
  1299.1 242.0 %copy-start.149 = (f32[768]{0:T(1024)S(1)}, f32[768]{0:T(1024)}, u32[]{:S(2)}) copy-start(f32[768]{0:T(1024)} %param.21) | copy-start | bytes 9220
  1299.1 242.0 %copy-start.169 = (f32[256]{0:T(256)S(1)}, f32[256]{0:T(256)}, u32[]{:S(2)}) copy-start(f32[256]{0:T(256)} %copy-done.168) | copy-start | bytes 3076
  1299.1 242.0 %copy-start.171 = (f32[256]{0:T(256)S(1)}, f32[256]{0:T(256)}, u32[]{:S(2)}) copy-start(f32[256]{0:T(256)} %copy-done.170) | copy-start | bytes 3076
  1299.1 242.0 %copy-start.173 = (f32[256]{0:T(256)S(1)}, f32[256]{0:T(256)}, u32[]{:S(2)}) copy-start(f32[256]{0:T(256)} %copy-done.172) | copy-start | bytes 3076
  1299.2 287.8 %all-gather.44.cloned.1.call-start = ((), (), s32[]{:S(2)}) async-start(), calls=%async_computation.40 | async-start | bytes 1966080 | tf_op jit(solution)/shard_map/all_gather | solution.py:287
  1549.7 75.4 %all-gather.52.cloned.1.call-start = ((), (), s32[]{:S(2)}) async-start(), calls=%async_computation.48 | async-start | bytes 1966080 | tf_op jit(solution)/shard_map/all_gather | solution.py:287
  1555.9 107.1 %all-gather.56.cloned.1.call-start = ((), (), s32[]{:S(2)}) async-start(), calls=%async_computation.52 | async-start | bytes 1966080 | tf_op jit(solution)/shard_map/all_gather | solution.py:287
  1557.6 143.0 %all-gather.48.cloned.1.call-start = ((), (), s32[]{:S(2)}) async-start(), calls=%async_computation.44 | async-start | bytes 1966080 | tf_op jit(solution)/shard_map/all_gather | solution.py:287
  1558.6 218.7 %reduce-scatter.38.cloned.1.call-start = ((), (), s32[]{:S(2)}) async-start(), calls=%async_computation.41 | async-start | bytes 3932160 | tf_op jit(solution)/shard_map/reduce_scatter | solution.py:289
  1600.2 225.3 %reduce-scatter.46.cloned.1.call-start = ((), (), s32[]{:S(2)}) async-start(), calls=%async_computation.49 | async-start | bytes 3932160 | tf_op jit(solution)/shard_map/reduce_scatter | solution.py:289
  1638.2 250.4 %reduce-scatter.50.cloned.1.call-start = ((), (), s32[]{:S(2)}) async-start(), calls=%async_computation.53 | async-start | bytes 3932160 | tf_op jit(solution)/shard_map/reduce_scatter | solution.py:289
  1676.3 275.0 %reduce-scatter.42.cloned.1.call-start = ((), (), s32[]{:S(2)}) async-start(), calls=%async_computation.45 | async-start | bytes 3932160 | tf_op jit(solution)/shard_map/reduce_scatter | solution.py:289
  1713.8 342.3 %reduce-scatter.56.cloned.1.call-start = ((), (), s32[]{:S(2)}) async-start(), calls=%async_computation.56 | async-start | bytes 2433024 | tf_op jit(solution)/shard_map/reduce_scatter | solution.py:332
  1720.4 440.4 %reduce-scatter.54.cloned.1.call-start = ((), (), s32[]{:S(2)}) async-start(), calls=%async_computation.55 | async-start | bytes 2433024 | tf_op jit(solution)/shard_map/reduce_scatter | solution.py:331
  1725.5 539.4 %reduce-scatter.52.cloned.1.call-start = ((), (), s32[]{:S(2)}) async-start(), calls=%async_computation.54 | async-start | bytes 2433024 | tf_op jit(solution)/shard_map/reduce_scatter | solution.py:330
  1777.2 111.4 %copy-start.67 = (f32[256,768]{1,0:T(8,128)S(1)}, f32[256,768]{1,0:T(8,128)}, u32[]{:S(2)}) copy-start(f32[256,768]{1,0:T(8,128)} %copy-done.66) | copy-start | bytes 2359300
  1777.2 111.4 %copy-start.217 = (f32[256]{0:T(256)S(1)}, f32[256]{0:T(256)}, u32[]{:S(2)}) copy-start(f32[256]{0:T(256)} %copy-done.216) | copy-start | bytes 3076
  1777.2 174.1 %copy-start.63 = (f32[256,768]{1,0:T(8,128)S(1)}, f32[256,768]{1,0:T(8,128)}, u32[]{:S(2)}) copy-start(f32[256,768]{1,0:T(8,128)} %get-tuple-element.87) | copy-start | bytes 2359300
  1777.2 174.1 %copy-start.219 = (f32[256]{0:T(256)S(1)}, f32[256]{0:T(256)}, u32[]{:S(2)}) copy-start(f32[256]{0:T(256)} %copy-done.218) | copy-start | bytes 3076
  1779.6 173.0 %copy-start.108 = (f32[256,768]{1,0:T(8,128)S(1)}, f32[256,768]{1,0:T(8,128)}, u32[]{:S(2)}) copy-start(f32[256,768]{1,0:T(8,128)} %add_add_fusion.14) | copy-start | bytes 2359300
  (210 other events, 1453.5 us)
Sparse Core Ops, SparseCore 0:
  13.5 39.7 all-gather.19
  55.5 35.9 all-gather.33
  93.1 35.9 all-gather.37
  130.5 35.9 all-gather.29
  168.6 59.0 reduce-scatter.19
  229.9 60.2 reduce-scatter.27
  292.5 60.2 reduce-scatter.31
  355.7 60.2 reduce-scatter.23
  423.0 37.1 all-gather.21
  462.2 35.9 all-gather.31
  501.0 59.0 reduce-scatter.21
  562.9 60.2 reduce-scatter.25
  626.9 37.0 all-gather.39
  666.7 52.9 all-gather.23
  722.4 53.0 all-gather.25
  777.4 36.0 all-gather.35
  816.1 52.9 all-gather.27
  871.9 59.1 reduce-scatter.33
  934.0 60.2 reduce-scatter.29
  1126.0 37.1 all-gather.49
  1178.8 37.1 all-gather.53
  1217.5 35.9 all-gather.45
  1255.1 35.9 all-gather.41
  1293.2 59.0 reduce-scatter.43
  1355.2 60.2 reduce-scatter.47
  1417.7 60.2 reduce-scatter.39
  1480.8 60.2 reduce-scatter.35
  1549.8 37.0 all-gather.43
  1589.1 35.9 all-gather.51
  1627.1 35.9 all-gather.55
  1664.6 35.9 all-gather.47
  1702.9 59.9 reduce-scatter.37
  1765.0 60.4 reduce-scatter.45
  1828.4 60.2 reduce-scatter.49
  1891.0 60.2 reduce-scatter.41
  1957.0 99.0 reduce-scatter.55
  2062.7 98.0 reduce-scatter.53
  2166.7 98.1 reduce-scatter.51
where the time goes:
time: 2280 us; the launch traced here: 2270 us
  waiting for transfers between devices  1620 us (71%)
  matrix products  355 us (16%)
  other arithmetic  109 us (5%)
  local copies, waits for them, and re-layouts  84.2 us (4%)
  blocking collectives  81.7 us (4%)
    reduce_scatter x16, waiting for transfers between devices, local(): lax.psum_scatter(producer(jnp.int32(0), amount * lax.axis_size('mp')), 'm...  865 us
    all_gather x16, waiting for transfers between devices, local(): lax.all_gather(values, 'mp', axis=0, tiled=True)  387 us
    reduce_scatter x1, waiting for transfers between devices, local(): lax.psum_scatter(totals[1], ('dp', 'mp'), scatter_dimension=1, tiled=True)  105 us
    reduce_scatter x1, waiting for transfers between devices, local(): lax.psum_scatter(totals[0], ('dp', 'mp'), scatter_dimension=1, tiled=True)  104 us
    reduce_scatter x1, waiting for transfers between devices, local(): lax.psum_scatter(totals[2], ('dp', 'mp'), scatter_dimension=1, tiled=True)  100 us
    unnamed x2, blocking collectives  81.7 us
    all_gather x1, waiting for transfers between devices, local(): lax.all_gather(joining_key, ('dp', 'mp'), axis=1, tiled=True)  52.5 us
  transfers between devices with their start and end apart: 38, of which 35 were waited for; matrix products, arithmetic and copies ran while one was open for 16% of the time, Pallas kernels for 0%

commit v1 on v0

v1 whole, which is shorter than its diff:
```python
import jax
import jax.numpy as jnp
from jax import lax
from jax.sharding import PartitionSpec as P

HEAD = 64
EPS = 1e-06
ROOT_HALF = 0.7071067811865476
INV_ROOT_2PI = 0.3989422804014327


def mm(a, b):
    return jnp.dot(a, b, preferred_element_type=jnp.float32)


def mm_nt(a, b):
    return lax.dot_general(a, b, (((1,), (1,)), ((), ())), preferred_element_type=jnp.float32)


def mm_tn(a, b):
    return lax.dot_general(a, b, (((0,), (0,)), ((), ())), preferred_element_type=jnp.float32)


def low(v):
    return v.astype(jnp.bfloat16)


def gelu_pair(x):
    cdf = 0.5 * (1.0 + lax.erf(x * ROOT_HALF))
    return x * cdf, cdf + x * (INV_ROOT_2PI * jnp.exp(-0.5 * x * x))


def normalize(v):
    center = v - jnp.mean(v, axis=-1, keepdims=True)
    r = lax.rsqrt(jnp.mean(center * center, axis=-1, keepdims=True) + EPS)
    return center * r, r


def norm_back(n, r, t):
    return r * (t - jnp.mean(t, axis=-1, keepdims=True) - n * jnp.mean(t * n, axis=-1, keepdims=True))


def local(
    tokens,
    segment_ids,
    row_ends,
    type_rows,
    ln1_gain,
    attn_qkv,
    attn_out,
    ffn_up,
    ffn_down,
    adapter_down,
    adapter_up,
    ln2_gain,
    joining_query,
    joining_key,
    joining_value,
    query_bias,
    cotangent,
):
    dp, mp = lax.axis_size("dp"), lax.axis_size("mp")
    dpi, mpi = lax.axis_index("dp"), lax.axis_index("mp")
    rows, width = tokens.shape
    seqs = row_ends.shape[0] // mp
    seq_len = rows // seqs
    adapters, _, bottle = adapter_down.shape
    factor = width ** (-0.5)
    scale = HEAD ** (-0.5)

    def share(mat):
        piece = mat.shape[0] // dp
        mine = lax.dynamic_slice_in_dim(mat, dpi * piece, piece, 0)
        return lax.all_gather(mine, ("mp", "dp"), axis=0, tiled=True)

    cols = attn_qkv.shape[2]
    qkv_all = share(jnp.transpose(attn_qkv, (1, 0, 2)).reshape(width, 3 * cols))
    qkv_all = qkv_all.reshape(mp, width, 3 * cols)
    out_all = share(attn_out)
    up_all = share(ffn_up).reshape(mp, width, ffn_up.shape[1])
    down_all = share(ffn_down).reshape(mp, ffn_down.shape[0], width)
    up_mat = adapter_up.reshape(adapters * bottle, width)
    dn_mat = jnp.transpose(adapter_down, (1, 0, 2)).reshape(width, adapters * bottle)

    own_q = jnp.transpose(joining_query)
    own_m = low(mm_nt(jnp.transpose(joining_key), up_mat))
    own_v = jnp.transpose(joining_value)
    q_t = lax.all_gather(own_q, ("dp", "mp"), axis=0, tiled=True)
    m_all = lax.all_gather(own_m, ("dp", "mp"), axis=0, tiled=True)
    v_t = lax.all_gather(own_v, ("dp", "mp"), axis=0, tiled=True)
    bias = lax.all_gather(query_bias, ("dp", "mp"), axis=0, tiled=True)
    w_mat = low(mm_tn(q_t, m_all))
    shift = mm(bias[None, :], m_all)

    own_types = lax.dynamic_slice_in_dim(segment_ids, mpi * rows, rows)
    ends = lax.dynamic_slice_in_dim(row_ends, mpi * seqs, seqs)
    type_f = type_rows.astype(jnp.float32)
    x = tokens.astype(jnp.float32) + jnp.where(
        own_types[:, None] == 1, type_f[1][None, :], type_f[0][None, :]
    )
    xb = low(x)
    heads = cols // HEAD
    proj = low(jnp.einsum("rd,zdc->zrc", xb, qkv_all, preferred_element_type=jnp.float32))
    pieces = proj.reshape(mp, seqs, seq_len, 3, heads, HEAD)
    q, k, v = pieces[:, :, :, 0], pieces[:, :, :, 1], pieces[:, :, :, 2]
    sc = jnp.einsum("zsqhd,zskhd->zshqk", q, k, preferred_element_type=jnp.float32) * scale
    places = lax.broadcasted_iota(jnp.int32, (1, 1, 1, 1, seq_len), 4)
    sc = jnp.where(places <= ends[None, :, None, None, None], sc, -1e30)
    e = jnp.exp(sc - jnp.max(sc, axis=-1, keepdims=True))
    probs = e / jnp.sum(e, axis=-1, keepdims=True)
    pb = low(probs)
    ctx = low(jnp.einsum("zshqk,zskhd->sqzhd", pb, v, preferred_element_type=jnp.float32))
    ctx2 = ctx.reshape(rows, width)
    n1, r1 = normalize(x + mm(ctx2, out_all))
    h1 = n1 * ln1_gain[None, :]
    h1b = low(h1)
    wide = jnp.einsum("rd,zdf->zrf", h1b, up_all, preferred_element_type=jnp.float32)
    act, act_back = gelu_pair(wide)
    act, act_back = low(act), low(act_back)
    merged = h1 + jnp.einsum("zrf,zfd->rd", act, down_all, preferred_element_type=jnp.float32)
    mb = low(merged)

    mid, mid_back = gelu_pair(mm(mb, dn_mat))
    ku = mm(mb, w_mat) + shift

    def group_sum(t):
        return jnp.sum(t.reshape(rows, adapters, bottle), axis=-1)

    def spread(t):
        return jnp.broadcast_to(t[:, :, None], (rows, adapters, bottle)).reshape(rows, adapters * bottle)

    jp = jax.nn.softmax(group_sum(mid * ku) * factor, axis=-1)
    mixed = low(merged + mm(low(spread(jp) * mid), up_mat))
    n2, r2 = normalize(merged + mm_nt(mixed, v_t))
    layer_out = n2 * ln2_gain[None, :]
    gc = norm_back(n2, r2, cotangent.astype(jnp.float32) * ln2_gain[None, :])
    gcb = low(gc)
    grad_value = mm_tn(mixed, gcb)
    gm = mm(gcb, v_t)
    gu = mm_nt(low(gm), up_mat)
    gp = group_sum(mid * gu)
    gs = jp * (gp - jnp.sum(jp * gp, axis=-1, keepdims=True)) * factor
    zb = low(spread(gs) * mid)
    big_r = mm_tn(zb, mb)
    small_s = jnp.sum(zb.astype(jnp.float32), axis=0)
    g_pre = low(mid_back * (spread(jp) * gu + spread(gs) * ku))
    g_merged = gc + gm + mm_nt(zb, w_mat) + mm_nt(g_pre, dn_mat)
    gmb = low(g_merged)
    g_act = jnp.einsum("rd,zfd->zrf", gmb, down_all, preferred_element_type=jnp.float32)
    g_wide = low(g_act * act_back)
    g_hid = g_merged + jnp.einsum("zrf,zdf->rd", g_wide, up_all, preferred_element_type=jnp.float32)
    g_sum = norm_back(n1, r1, g_hid * ln1_gain[None, :])
    g_ctx = low(mm_nt(low(g_sum), out_all)).reshape(seqs, seq_len, mp, heads, HEAD)
    delta = jnp.sum(
        g_ctx.astype(jnp.float32) * ctx.astype(jnp.float32), axis=-1
    )
    gpr = jnp.einsum("sqzhd,zskhd->zshqk", g_ctx, v, preferred_element_type=jnp.float32)
    ds = low(pb.astype(jnp.float32) * (gpr - jnp.transpose(delta, (2, 0, 3, 1))[..., None]))
    gv = low(jnp.einsum("zshqk,sqzhd->zskhd", pb, g_ctx, preferred_element_type=jnp.float32))
    gq = low(jnp.einsum("zshqk,zskhd->zsqhd", ds, k, preferred_element_type=jnp.float32) * scale)
    gk = low(jnp.einsum("zshqk,zsqhd->zskhd", ds, q, preferred_element_type=jnp.float32) * scale)
    g_proj = jnp.stack((gq, gk, gv), axis=3).reshape(mp, rows, 3 * cols)
    g_in = g_sum + jnp.einsum("zrc,zdc->rd", g_proj, qkv_all, preferred_element_type=jnp.float32)

    g_value = lax.psum_scatter(jnp.transpose(low(grad_value)), ("dp", "mp"), scatter_dimension=0, tiled=True)
    packed = jnp.concatenate((low(big_r), low(small_s)[None, :], jnp.zeros((15, width), jnp.bfloat16)))
    total = lax.psum(packed, ("dp", "mp"))
    big_r, small_s = total[:width], total[width]
    g_query = mm_tn(big_r, jnp.transpose(own_m))
    inner = mm(big_r, joining_query) + small_s.astype(jnp.float32)[:, None] * query_bias.astype(jnp.float32)[None, :]
    g_key = mm_tn(up_mat, low(inner))
    g_bias = mm(own_m, small_s[:, None])[:, 0]
    return (layer_out, g_in, g_query, g_key, jnp.transpose(g_value).astype(jnp.float32), g_bias)


def solution(mesh):
    in_specs = (
        P(("dp", "mp"), None),
        P("dp"),
        P("dp"),
        P(),
        P(),
        P(None, None, "mp"),
        P("mp", None),
        P(None, "mp"),
        P("mp", None),
        P(),
        P(),
        P(),
        P(None, ("dp", "mp")),
        P(None, ("dp", "mp")),
        P(None, ("dp", "mp")),
        P(("dp", "mp")),
        P(("dp", "mp"), None),
    )
    out_specs = (
        P(("dp", "mp"), None),
        P(("dp", "mp"), None),
        P(None, ("dp", "mp")),
        P(None, ("dp", "mp")),
        P(None, ("dp", "mp")),
        P(("dp", "mp")),
    )
    return jax.shard_map(local, mesh=mesh, in_specs=in_specs, out_specs=out_specs, check_vma=False)
```

time: 2280 us -> 769 us (0.34)
  waiting for transfers between devices: 1620 us -> 450 us
  matrix products: 355 us -> 146 us
  other arithmetic: 109 us -> 41.3 us
  blocking collectives: 81.7 us -> 42.1 us
    reduce_scatter x19 -> x1, waiting for transfers between devices: 1170 us -> 94.7 us  [local(): lax.psum_scatter(jnp.transpose(low(grad_value)), ('dp', 'mp'), scatter_di...]
    dot_general x112 -> x29, matrix products: 350 us -> 146 us  [the longest x1 22.3 us: local(): jnp.einsum('zrf,zdf->rd', g_wide, up_all, preferred_element_type=jnp.floa...]
    all_gather x19 -> x7, waiting for transfers between devices: 441 us -> 266 us  [the longest x4 180 us: share(): return lax.all_gather(mine, ('mp', 'dp'), axis=0, tiled=True)]
    psum x0 -> x1, waiting for transfers between devices: none -> 87.4 us  [local(): total = lax.psum(packed, ('dp', 'mp'))]
    unnamed x2 -> x1, blocking collectives: 81.7 us -> 42.1 us
    reduce_sum x23 -> x9, other arithmetic: 45 us -> 12.3 us  [the longest x2 4.63 us: group_sum(): return jnp.sum(t.reshape(rows, adapters, bottle), axis=-1)]
  transfers between devices with their start and end apart: 38 -> 9, of which waited for: 35 -> 9; matrix products, arithmetic and copies ran while one was open for 16% -> 20% of each run, Pallas kernels for 0% -> 0%
where the time goes in v1:
time: 769 us; the launch traced here: 758 us
  waiting for transfers between devices  450 us (59%)
  matrix products  146 us (19%)
  local copies, waits for them, and re-layouts  63.5 us (8%)
  blocking collectives  42.1 us (5%)
  other arithmetic  41.3 us (5%)
  between operations  14.5 us (2%)
    all_gather x4, waiting for transfers between devices, share(): return lax.all_gather(mine, ('mp', 'dp'), axis=0, tiled=True)  180 us
    reduce_scatter x1, waiting for transfers between devices, local(): lax.psum_scatter(jnp.transpose(low(grad_value)), ('dp', 'mp'), scatter_di...  94.7 us
    psum x1, waiting for transfers between devices, local(): total = lax.psum(packed, ('dp', 'mp'))  87.4 us
    all_gather x1, waiting for transfers between devices, local(): q_t = lax.all_gather(own_q, ('dp', 'mp'), axis=0, tiled=True)  54.2 us
    unnamed x1, blocking collectives  42.1 us
    all_gather x1, waiting for transfers between devices, local(): v_t = lax.all_gather(own_v, ('dp', 'mp'), axis=0, tiled=True)  30.8 us
    dot_general x1, matrix products, local(): jnp.einsum('zrf,zdf->rd', g_wide, up_all, preferred_element_type=jnp.floa...  22.3 us
    unnamed x86, local copies, waits for them, and re-layouts  22.2 us
  transfers between devices with their start and end apart: 9, of which 9 were waited for; matrix products, arithmetic and copies ran while one was open for 20% of the time, Pallas kernels for 0%

profile of v1, /device:TPU:0, one launch (start us, length us, event | category | flops | bytes accessed | tf_op | source)
XLA Modules:
  0.0 757.6 jit_solution(11620015231173208338)
XLA Ops:
  8.4 1.9 convolution_convert_fusion.5
  13.1 1.4 constant_dynamic-slice_fusion.2
  14.6 1.6 constant_dynamic-slice_fusion.1
  16.2 1.6 constant_dynamic-slice_fusion
  19.4 1.6 copy.107
  21.9 42.1 %all-reduce = bf16[768]{0:T(1024)(128)(2,1)S(1)} all-reduce(bf16[768]{0:T(1024)(128)(2,1)S(1)} %dynamic-update-slice), channel_id=1, replica_groups=mesh['dp'=8,'mp'=4] {'dp','mp'}, use_global_device_ids=true, to_apply=%add | all-reduce | flops 768 | bytes 3072
  64.0 1.7 copy.122
  68.4 1.6 convolution_reduce_fusion
  69.9 54.2 %all-gather.18.cloned.1.call-done = bf16[768,768]{1,0:T(8,128)(2,1)} async-done(((bf16[24,768]{1,0:T(8,128)(2,1)}), bf16[768,768]{1,0:T(8,128)(2,1)}) %all-gather.18.cloned.1.call-update) | async-done | bytes 1179664 | tf_op jit(solution)/shard_map/all_gather | solution.py:88
  124.1 3.8 convolution_convert_fusion.4
  127.9 59.8 %all-gather.8.cloned.1.call-done = bf16[3072,576]{1,0:T(8,128)(2,1)} async-done(((bf16[96,576]{1,0:T(8,128)(2,1)}), bf16[3072,576]{1,0:T(8,128)(2,1)}) %all-gather.8.cloned.1.call-update) | async-done | bytes 3538960 | tf_op jit(solution)/shard_map/all_gather | solution.py:74
  187.7 8.8 %convert_bitcast_fusion = bf16[4,1024,576]{1,2,0:T(8,128)(2,1)} fusion(bf16[4,768,576]{2,1,0:T(8,128)(2,1)} %bitcast.200, bf16[1024,768]{0,1:T(8,128)(2,1)} %copy.107, f32[768]{0:T(1024)S(1)} %get-tuple-element.35, f32[768]{0:T(1024)S(1)} %get-tuple-element.34, pred[1024]{0:T(1024)(128)(4,1)S(1)} %dynamic-slice_compare_fusion), kind=kOutput, calls=%fused_computation.35 | convolution fusion | flops 3629383680 | bytes 9837568 | tf_op jit(solution)/shard_map/rd,zdc->zrc/dot_general | solution.py:103
  196.5 8.9 %reshape.225 = bf16[4,4,256,3,3,64]{2,1,5,4,3,0:T(4,128)(2,1)} reshape(bf16[4,1024,576]{1,2,0:T(8,128)(2,1)} %convert_bitcast_fusion) | data formatting | bytes 9437184 | tf_op jit(solution)/shard_map/reshape | solution.py:104
  205.4 3.3 fusion.107
  210.4 1.8 fusion.73
  212.2 8.3 %fusion.108 = (f32[4,4,3,256]{3,2,1,0:T(4,128)S(1)}, f32[4,4,3,256,256]{3,4,2,1,0:T(8,128)}) fusion(f32[4,4,3,256,256]{3,4,2,1,0:T(8,128)S(1)} %fusion.73, pred[4,256]{1,0:T(4,128)(4,1)S(1)} %iota_compare_fusion), kind=kOutput, calls=%fused_computation.160 | output fusion | flops 18874624 | bytes 25216000 | tf_op jit(solution)/shard_map/sub | solution.py:109
  220.5 8.9 %divide_convert_fusion = bf16[4,4,3,256,256]{3,4,2,1,0:T(8,128)(2,1)} fusion(f32[4,4,3,256,256]{3,4,2,1,0:T(8,128)} %get-tuple-element.45, f32[4,4,3,256]{3,2,1,0:T(4,128)S(1)} %get-tuple-element.44), kind=kLoop, calls=%fused_computation.16 | loop fusion | flops 6291456 | bytes 18923520 | tf_op jit(solution)/shard_map/convert_element_type | solution.py:25
  229.4 3.9 fusion.67
  235.7 1.5 copy.166
  237.2 6.6 all-gather.10.cloned.1.call-done
  243.8 4.0 fusion.109
  247.8 1.6 copy-done.21
  249.9 59.3 %all-gather.12.cloned.1.call-done = bf16[3072,768]{1,0:T(8,128)(2,1)} async-done(((bf16[96,768]{1,0:T(8,128)(2,1)}), bf16[3072,768]{1,0:T(8,128)(2,1)}) %all-gather.12.cloned.1.call-update) | async-done | bytes 4718608 | tf_op jit(solution)/shard_map/all_gather | solution.py:74
  309.2 10.9 %fusion.48 = f32[4,768,1024]{2,1,0:T(8,128)} fusion(bf16[4,768,768]{2,1,0:T(8,128)(2,1)} %bitcast.196, f32[1024,768]{0,1:T(8,128)} %copy-done.21, f32[768]{0:T(1024)S(1)} %copy-done.34, f32[1024]{0:T(1024)S(1)} %add_rsqrt_fusion.1, f32[1024]{0:T(1024)S(1)} %broadcast_multiply_fusion.5), kind=kOutput, calls=%fused_computation.77 | convolution fusion | flops 4834983936 | bytes 20458496 | tf_op jit(solution)/shard_map/rd,zdf->zrf/dot_general | solution.py:117
  320.1 54.3 %all-gather.14.cloned.1.call-done = bf16[3072,768]{1,0:T(8,128)(2,1)} async-done(((bf16[96,768]{1,0:T(8,128)(2,1)}), bf16[3072,768]{1,0:T(8,128)(2,1)}) %all-gather.14.cloned.1.call-update) | async-done | bytes 4718608 | tf_op jit(solution)/shard_map/all_gather | solution.py:74
  374.4 10.2 %bitcast_add_fusion.2 = f32[1024,768]{0,1:T(8,128)S(1)} fusion(f32[1024,768]{0,1:T(8,128)} %copy-done.21, bf16[4,768,768]{2,1,0:T(8,128)(2,1)} %bitcast.198, f32[4,768,1024]{2,1,0:T(8,128)} %fusion.48, f32[768]{0:T(1024)S(1)} %copy-done.34, f32[1024]{0:T(1024)S(1)} %add_rsqrt_fusion.1, f32[1024]{0:T(1024)S(1)} %broadcast_multiply_fusion.5), kind=kOutput, calls=%fused_computation.49 | convolution fusion | flops 4850712576 | bytes 23604224 | tf_op jit(solution)/shard_map/zrf,zfd->rd/dot_general | solution.py:120
  384.6 1.4 fusion.94
  386.8 4.7 add_multiply_fusion.1
  391.5 2.3 reduce_sum.141
  394.0 2.5 fusion.32
  396.7 2.6 add_convert_fusion
  399.3 30.8 %all-gather.20.cloned.1.call-done = bf16[768,768]{1,0:T(8,128)(2,1)} async-done(((bf16[24,768]{1,0:T(8,128)(2,1)}), bf16[768,768]{1,0:T(8,128)(2,1)}) %all-gather.20.cloned.1.call-update) | async-done | bytes 1179664 | tf_op jit(solution)/shard_map/all_gather | solution.py:90
  430.1 4.1 fusion.110
  435.0 2.5 fusion.36
  437.5 2.0 fusion.82
  439.5 4.0 fusion.111
  443.6 2.3 reduce_sum.147
  446.0 2.4 fusion.104
  448.7 2.4 convolution_convert_fusion.3
  451.2 1.5 fusion.114
  454.1 2.2 fusion.31
  457.2 4.2 add_add_fusion
  461.4 22.3 %fusion.103 = (f32[1024]{0:T(1024)S(1)}, f32[1024]{0:T(1024)S(1)}, f32[1024,768]{0,1:T(8,128)}) fusion(f32[1024]{0:T(1024)S(1)} %add_rsqrt_fusion.1, f32[1024,768]{0,1:T(8,128)} %copy-done.21, f32[1024]{0:T(1024)S(1)} %broadcast_multiply_fusion.5, f32[768]{0:T(1024)S(1)} %copy-done.34, f32[1024,768]{0,1:T(8,128)} %add_add_fusion, ...), kind=kOutput, calls=%fused_computation.157 | convolution fusion | flops 9707714560 | bytes 31476736 | tf_op jit(solution)/shard_map/zrf,zdf->rd/dot_general | solution.py:151
  483.7 5.2 convolution_convert_fusion.1
  488.9 1.6 copy.125
  490.5 2.9 reshape.235
  493.4 2.0 multiply_reduce_fusion
  495.4 8.2 %multiply_convert_fusion = bf16[4,4,3,256,256]{3,4,2,1,0:T(8,128)(2,1)} fusion(bf16[4,4,3,256,256]{3,4,2,1,0:T(8,128)(2,1)} %divide_convert_fusion, bf16[4,4,256,1,3,64]{2,1,5,4,3,0:T(4,128)(2,1)} %copy-done.17, bf16[4,256,4,3,64]{1,0,4,3,2:T(4,128)(2,1)S(1)} %reshape.235, f32[4,256,4,3]{1,3,2,0:T(4,128)S(1)} %multiply_reduce_fusion), kind=kOutput, calls=%fused_computation.15 | convolution fusion | flops 415236096 | bytes 15777792 | tf_op jit(solution)/shard_map/sqzhd,zskhd->zshqk/dot_general | solution.py:157
  503.6 5.6 fusion.71
  509.1 4.9 fusion.72
  514.1 3.2 fusion.70
  519.0 2.3 pad_maximum_fusion
  521.3 6.6 copy.135
  527.9 8.8 %reshape.236 = bf16[4,1024,576]{1,2,0:T(8,128)(2,1)} reshape(bf16[4,4,256,3,3,64]{2,1,5,4,3,0:T(4,128)(2,1)} %copy.135) | data formatting | bytes 9437184 | tf_op jit(solution)/shard_map/reshape | solution.py:162
  536.8 5.4 convolution_convert_fusion.2
  542.2 11.2 %bitcast_add_fusion = f32[1024,768]{0,1:T(8,128)} fusion(bf16[4,768,576]{2,1,0:T(8,128)(2,1)} %bitcast.201, bf16[4,1024,576]{1,2,0:T(8,128)(2,1)} %reshape.236, f32[1024]{0:T(1024)S(1)} %broadcast_multiply_fusion, f32[1024,768]{0,1:T(8,128)} %copy-done.21, f32[1024]{0:T(1024)S(1)} %broadcast_multiply_fusion.5, f32[1024,768]{0,1:T(8,128)} %get-tuple-element.53, ...), kind=kOutput, calls=%fused_computation.46 | convolution fusion | flops 3629383680 | bytes 17711104 | tf_op jit(solution)/shard_map/zrc,zdc->rd/dot_general | solution.py:163
  553.3 3.5 copy.139
  556.9 3.6 copy.138
  560.5 87.4 %all-reduce.3.cloned.1.call-done = bf16[784,768]{1,0:T(8,128)(2,1)} async-done(((bf16[784,768]{1,0:T(8,128)(2,1)}), bf16[784,768]{1,0:T(8,128)(2,1)}) %all-reduce.3.cloned.1.call-update) | async-done | bytes 1204240 | tf_op jit(solution)/shard_map/psum | solution.py:167
  648.6 1.3 convolution_bitcast_fusion.1
  649.9 2.2 fusion.79
  652.1 2.6 convolution_bitcast_fusion
  654.7 94.7 %reduce-scatter.2.cloned.1.call-done = bf16[24,768]{1,0:T(8,128)(2,1)} async-done(((bf16[768,768]{1,0:T(8,128)(2,1)}), bf16[24,768]{1,0:T(8,128)(2,1)}) %reduce-scatter.2.cloned.1.call-update) | async-done | bytes 36880 | tf_op jit(solution)/shard_map/reduce_scatter | solution.py:165
  749.4 1.4 convert_bitcast_fusion.1
  (129 shorter events, 20.7 us)
Async XLA Ops:
  7.2 1.3 copy-start
  7.2 12.2 %copy-start.22 = (bf16[1024,768]{1,0:T(8,128)(2,1)S(1)}, bf16[1024,768]{1,0:T(8,128)(2,1)}, u32[]{:S(2)}) copy-start(bf16[1024,768]{1,0:T(8,128)(2,1)} %param.17) | copy-start | bytes 4718596
  7.2 61.2 %all-gather.16.cloned.1.call-start = ((), (), s32[]{:S(2)}) async-start(), calls=%async_computation.5 | async-start | bytes 1216512 | tf_op jit(solution)/shard_map/all_gather | solution.py:89
  8.4 12.5 %copy-start.35 = (s32[16]{0:T(128)S(1)}, s32[16]{0:T(128)}, u32[]{:S(2)}) copy-start(s32[16]{0:T(128)} %param.19) | copy-start | bytes 196
  8.4 12.7 %copy-start.36 = (bf16[24]{0:T(256)(128)(2,1)S(1)}, bf16[24]{0:T(256)(128)(2,1)}, u32[]{:S(2)}) copy-start(bf16[24]{0:T(256)(128)(2,1)} %param.32) | copy-start | bytes 148
  10.3 113.8 %all-gather.18.cloned.1.call-start = ((), (), s32[]{:S(2)}) async-start(), calls=%async_computation.6 | async-start | bytes 1216512 | tf_op jit(solution)/shard_map/all_gather | solution.py:88
  11.1 176.6 %all-gather.8.cloned.1.call-start = ((), (), s32[]{:S(2)}) async-start(), calls=%async_computation.1 | async-start | bytes 4055040 | tf_op jit(solution)/shard_map/all_gather | solution.py:74
  13.0 230.8 %all-gather.10.cloned.1.call-start = ((), (), s32[]{:S(2)}) async-start(), calls=%async_computation.2 | async-start | bytes 1216512 | tf_op jit(solution)/shard_map/all_gather | solution.py:74
  14.5 294.7 %all-gather.12.cloned.1.call-start = ((), (), s32[]{:S(2)}) async-start(), calls=%async_computation.3 | async-start | bytes 4866048 | tf_op jit(solution)/shard_map/all_gather | solution.py:74
  16.2 358.2 %all-gather.14.cloned.1.call-start = ((), (), s32[]{:S(2)}) async-start(), calls=%async_computation.4 | async-start | bytes 4866048 | tf_op jit(solution)/shard_map/all_gather | solution.py:74
  17.8 412.3 %all-gather.20.cloned.1.call-start = ((), (), s32[]{:S(2)}) async-start(), calls=%async_computation.7 | async-start | bytes 1216512 | tf_op jit(solution)/shard_map/all_gather | solution.py:90
  18.6 629.3 %all-reduce.3.cloned.1.call-start = ((), (), s32[]{:S(2)}) async-start(), calls=%async_computation.8 | async-start | bytes 2408448 | tf_op jit(solution)/shard_map/psum | solution.py:167
  65.7 390.6 %copy-start.7 = (bf16[1024,768]{0,1:T(8,128)(2,1)}, bf16[1024,768]{0,1:T(8,128)(2,1)S(1)}, u32[]{:S(2)}) copy-start(bf16[1024,768]{0,1:T(8,128)(2,1)S(1)} %copy.122) | copy-start | bytes 4718596
  208.7 1.2 copy-start.5
  208.7 1.7 copy-start.6
  208.7 20.6 %copy-start.17 = (bf16[4,4,256,1,3,64]{2,1,5,4,3,0:T(4,128)(2,1)}, bf16[4,4,256,1,3,64]{2,1,5,4,3,0:T(4,128)(2,1)S(1)}, u32[]{:S(2)}) copy-start(bf16[4,4,256,1,3,64]{2,1,5,4,3,0:T(4,128)(2,1)S(1)} %get-tuple-element.40) | copy-start | bytes 4718596
  233.3 1.2 copy-start.16
  247.8 1.7 copy-start.21
  247.8 61.4 %copy-start.34 = (f32[768]{0:T(1024)S(1)}, f32[768]{0:T(1024)}, u32[]{:S(2)}) copy-start(f32[768]{0:T(1024)} %param.21) | copy-start | bytes 9220
  374.4 10.2 %copy-start.26 = (bf16[16,768,48]{1,2,0:T(8,128)(2,1)S(1)}, bf16[16,768,48]{1,2,0:T(8,128)(2,1)}, u32[]{:S(2)}) copy-start(bf16[16,768,48]{1,2,0:T(8,128)(2,1)} %param.26) | copy-start | bytes 3538948
  384.6 1.7 copy-start.18
  384.6 2.2 copy-start.23
  386.8 4.7 copy-start.9
  393.9 2.8 copy-start.19
  434.3 3.3 copy-start.3
  434.3 0.7 copy-start.30
  435.0 2.5 copy-start.33
  437.5 2.0 copy-start.2
  439.5 4.1 copy-start.13
  445.9 2.8 copy-start.20
  448.7 2.5 copy-start.24
  448.7 4.0 copy-start.12
  451.2 1.9 copy-start.10
  451.2 2.8 copy-start.11
  454.0 2.2 copy-start.4
  454.0 2.8 copy-start.14
  454.0 3.1 copy-start.27
  503.5 5.6 copy-start.1
  503.5 10.5 %slice-start = ((s8[6291456]{0:T(1024)(128)(4,1)}), s8[4194304]{0:T(1024)(128)(4,1)S(1)}, s32[]{:S(2)}) async-start(s8[6291456]{0:T(1024)(128)(4,1)} %bitcast.185), calls=%async_computation.10 | async-start | bytes 8388608
  509.1 4.9 slice-start.1
  514.0 3.2 copy-start.25
  514.0 3.2 copy-start.31
  517.2 1.8 copy-start.15
  518.6 230.9 %reduce-scatter.2.cloned.1.call-start = ((), (), s32[]{:S(2)}) async-start(), calls=%async_computation.9 | async-start | bytes 1216512 | tf_op jit(solution)/shard_map/reduce_scatter | solution.py:165
  527.9 8.8 %copy-start.8 = (bf16[1024,768]{0,1:T(8,128)(2,1)S(1)}, bf16[1024,768]{0,1:T(8,128)(2,1)}, u32[]{:S(2)}) copy-start(bf16[1024,768]{0,1:T(8,128)(2,1)} %copy-done.7) | copy-start | bytes 4718596
  556.9 91.7 %copy-start.28 = (bf16[24,768]{1,0:T(8,128)(2,1)S(1)}, bf16[24,768]{1,0:T(8,128)(2,1)}, u32[]{:S(2)}) copy-start(bf16[24,768]{1,0:T(8,128)(2,1)} %convolution_convert_fusion.5) | copy-start | bytes 110596
  556.9 95.2 %copy-start.29 = (bf16[768,24]{0,1:T(8,128)(2,1)S(1)}, bf16[768,24]{0,1:T(8,128)(2,1)}, u32[]{:S(2)}) copy-start(bf16[768,24]{0,1:T(8,128)(2,1)} %param.29) | copy-start | bytes 110596
  556.9 95.2 %copy-start.32 = (f32[24]{0:T(128)S(1)}, f32[24]{0:T(128)}, u32[]{:S(2)}) copy-start(f32[24]{0:T(128)} %convert_element_type.175) | copy-start | bytes 292
Sparse Core Ops, SparseCore 0:
  11.4 56.9 all-gather.15
  71.1 52.9 all-gather.17
  127.6 60.1 all-gather.7
  191.1 52.6 all-gather.9
  246.5 62.5 all-gather.11
  311.9 62.4 all-gather.13
  377.2 52.8 all-gather.19
  518.7 129.1 all-reduce.2
  652.9 96.4 reduce-scatter.1
